TPU v7x, 32 devices: a whole 2x2x4 slice. The times are simulated.
32 devices in a mesh: strip: 2 (over x), ifg: 16 (over z, y, core).
Axes of the slice: x: 2, y: 2, z: 4, core: 2. Of those that a mesh axis runs over, the one named last changes fastest.
Arguments:
- phases: bfloat16 [1024, 128, 512], P('ifg', 'strip'), parts along dimension 1, may hold values from -9 to 9
- coherence: int32 [8, 32], P('strip'), parts along dimension 0, may hold values from 0 to 1
- date_pairs: int32 [1024, 2], replicated, may hold values from 0 to 255
- ramp_inverse: bfloat16 [1024, 1024], replicated, as said below
- pseudo_inverse: bfloat16 [256, 1024], replicated, may hold values from -0.1875 to 0.1875
Outputs:
- displacement: float32 [256, 128, 512], P(None, ('strip', 'ifg')), parts along dimension 1
- residual_phase: bfloat16 [1024, 128, 512], P('ifg', 'strip'), parts along dimension 1
There are 2 independent parts, one for each index of `strip`. A program takes and returns all parts, laid end to end along the dimension named above; an argument that names none is the same for every part. Nothing has to cross between parts.
Inputs may be any that keep to these rules, and one draw needn't show every extreme that they name: `ramp_inverse`: full rank.
All inputs are finite; a program needn't handle non-finite values.
Results may differ from a plain program's by a relative error of at most 0.0049.
Values may be sent and summed in bfloat16 or wider, within the bound.
A program may use at most 128 MiB of HBM per device.

v0:
```python
import jax
import jax.numpy as jnp
from jax import lax
from jax.sharding import PartitionSpec as P

KNOTS = 32
BLOCK = 16


highest = lax.Precision.HIGHEST


def spline_basis(count, knot_count):
    spacing = (knot_count - 3) / (count - 1)
    places = jnp.arange(count, dtype=jnp.float32) * spacing
    centres = jnp.arange(knot_count, dtype=jnp.float32) - 1.0
    offset = jnp.abs(places[:, None] - centres[None, :])
    inner = 2.0 / 3.0 - offset * offset + 0.5 * offset**3
    outer = (2.0 - offset) ** 3 / 6.0
    return jnp.where(offset < 1.0, inner, jnp.where(offset < 2.0, outer, 0.0))


def weight_field(coherence):
    block_rows, block_cols = coherence.shape
    spread = jnp.broadcast_to(
        coherence.astype(jnp.float32)[:, None, :, None], (block_rows, BLOCK, block_cols, BLOCK)
    )
    return spread.reshape(block_rows * BLOCK, block_cols * BLOCK)


def evaluate_ramp(left_basis, coefficients, col_basis):
    ramp_rows = jnp.einsum("ra,iab->irb", left_basis, coefficients, precision=highest)
    return jnp.einsum("irb,cb->irc", ramp_rows, col_basis, precision=highest)


def per_device(phases, coherence, date_pairs, ramp_inverse, pseudo_inverse):
    local_count, row_count, col_count = phases.shape
    knot_count = KNOTS
    square = knot_count * knot_count
    devices = lax.axis_size("ifg")
    row_share = row_count // devices
    row_basis = spline_basis(row_count, knot_count)
    col_basis = spline_basis(col_count, knot_count)
    weight = weight_field(coherence)
    masked = phases.astype(jnp.float32) * weight
    partial_score = jnp.einsum("irc,cb->irb", masked, col_basis, precision=highest)
    score = jnp.einsum("ra,irb->iab", row_basis, partial_score, precision=highest)
    solved = jnp.dot(
        ramp_inverse.astype(jnp.float32), score.reshape(local_count, square).T, precision=highest
    )
    coefficients = solved.T
    ramp = evaluate_ramp(
        row_basis, coefficients.reshape(local_count, knot_count, knot_count), col_basis
    )
    payload = (phases.astype(jnp.float32) - ramp).astype(jnp.bfloat16)
    regrouped = lax.all_to_all(payload, "ifg", split_axis=1, concat_axis=0, tiled=True)
    total_count = regrouped.shape[0]
    flat = regrouped.reshape(total_count, row_share * col_count)
    displacement = jnp.dot(pseudo_inverse, flat, preferred_element_type=jnp.float32)
    displacement = displacement.reshape(pseudo_inverse.shape[0], row_share, col_count)
    later = jnp.take(displacement, date_pairs[:, 1], axis=0)
    earlier = jnp.take(displacement, date_pairs[:, 0], axis=0)
    residual_band = (regrouped.astype(jnp.float32) - (later - earlier)).astype(jnp.bfloat16)
    residual_phase = lax.all_to_all(residual_band, "ifg", split_axis=0, concat_axis=1, tiled=True)
    return (displacement, residual_phase)


def solution(mesh):
    placed = (P("ifg", "strip", None), P("strip", None), P(), P(), P())
    return jax.shard_map(
        per_device,
        mesh=mesh,
        in_specs=placed,
        out_specs=(P(None, ("strip", "ifg"), None), P("ifg", "strip", None)),
        check_vma=False,
    )
```

profile of v0, /device:TPU:1, one launch (start us, length us, event | category | flops | bytes accessed | tf_op | source)
XLA Modules:
  0.0 301.5 jit_solution(410642860547793922)
XLA Ops:
  0.6 0.0 copy-start
  0.7 0.8 convert_element_type.21
  1.5 0.2 broadcast_in_dim.27
  1.7 0.6 mul.60
  2.3 13.4 %fusion = f32[64,64,32]{1,2,0:T(8,128)S(1)} fusion(bf16[64,64,512]{2,1,0:T(8,128)(2,1)} %param.7, f32[64,512]{1,0:T(8,128)S(1)} %mul.60, f32[32]{0:T(128)S(1)} %iota_add_fusion, f32[512]{0:T(512)S(1)} %iota_multiply_fusion), kind=kOutput, calls=%fused_computation.4 | convolution fusion | flops 809746432 | bytes 4851840 | tf_op jit(solution)/shard_map/irc,cb->irb/dot_general | solution.py:46
  15.7 3.1 %convolution_bitcast_fusion.1 = f32[64,32,32]{0,1,2:T(8,128)S(1)} fusion(f32[64,64,32]{1,2,0:T(8,128)S(1)} %fusion, f32[32]{0:T(128)S(1)} %iota_add_fusion, f32[64]{0:T(128)S(1)} %iota_multiply_fusion.1), kind=kOutput, calls=%fused_computation.11 | convolution fusion | flops 50362368 | bytes 786816 | tf_op jit(solution)/shard_map/ra,irb->iab/dot_general | solution.py:47
  18.9 0.3 copy.44
  19.2 0.0 copy-done
  19.2 1.8 fusion.90
  21.0 0.9 copy.46
  22.0 1.0 convolution_bitcast_fusion
  23.0 9.0 %fusion.1 = bf16[64,64,512]{2,1,0:T(8,128)(2,1)S(1)} fusion(bf16[64,64,512]{2,1,0:T(8,128)(2,1)} %param.7, f32[64,64,32]{1,2,0:T(8,128)S(1)} %convolution_bitcast_fusion, f32[32]{0:T(128)S(1)} %iota_add_fusion, f32[512]{0:T(512)S(1)} %iota_multiply_fusion), kind=kOutput, calls=%fused_computation.5 | convolution fusion | flops 811843584 | bytes 8915072 | tf_op jit(solution)/shard_map/irb,cb->irc/dot_general | solution.py:33
  32.0 4.4 %copy.47 = bf16[64,64,512]{2,0,1:T(8,128)(2,1)} copy(bf16[64,64,512]{2,1,0:T(8,128)(2,1)S(1)} %fusion.1) | data formatting | bytes 8388608 | tf_op jit(solution)/shard_map/convert_element_type | solution.py:55
  36.4 7.5 %all-to-all-start = ((bf16[64,64,512]{2,0,1:T(8,128)(2,1)}), bf16[64,64,512]{2,0,1:T(8,128)(2,1)}, u32[]{:S(2)}, u32[]{:S(2)}) async-start(bf16[64,64,512]{2,0,1:T(8,128)(2,1)} %copy.47), calls=%async_computation | async-start | bytes 8388608 | tf_op jit(solution)/shard_map/all_to_all | solution.py:56
  43.9 0.0 copy-done.3
  44.0 78.0 %all-to-all-done = bf16[64,64,512]{2,0,1:T(8,128)(2,1)} async-done(((bf16[64,64,512]{2,0,1:T(8,128)(2,1)}), bf16[64,64,512]{2,0,1:T(8,128)(2,1)}, u32[]{:S(2)}, u32[]{:S(2)}) %all-to-all-start) | async-done | bytes 4194336 | tf_op jit(solution)/shard_map/all_to_all | solution.py:56
  122.0 5.7 %copy.48 = bf16[16,64,4,512]{3,2,1,0:T(4,128)(2,1)S(1)} copy(bf16[16,64,4,512]{3,1,2,0:T(8,128)(2,1)} %bitcast.8) | data formatting | bytes 8388608 | tf_op jit(solution)/shard_map/all_to_all | solution.py:56
  127.7 6.6 %copy.49 = f32[16,64,4,512]{3,1,0,2:T(8,128)} copy(bf16[16,64,4,512]{3,1,2,0:T(8,128)(2,1)} %bitcast.8) | data formatting | bytes 12582912 | tf_op jit(solution)/shard_map/convert_element_type | solution.py:63
  134.3 1.4 copy.59
  135.7 0.0 copy-done.4
  135.8 2.7 fusion.91
  138.5 2.2 copy.55
  140.7 0.0 copy-start.2
  140.7 13.3 %gather_fusion.1 = f32[1024,4,512]{2,1,0:T(4,128)} fusion(f32[256,4,512]{2,1,0:T(4,128)S(1)} %copy.55, s32[1024]{0:T(1024)S(1)} %fusion.64), kind=kCustom, calls=%fused_computation.1.clone | custom fusion | bytes 16781312 | tf_op jit(solution)/shard_map/jit(_take)/gather | solution.py:62
  154.0 0.0 copy-done.2
  154.0 13.3 %gather_fusion = f32[1024,4,512]{2,1,0:T(4,128)} fusion(f32[256,4,512]{2,1,0:T(4,128)S(1)} %copy.55, s32[1024]{0:T(1024)S(1)} %fusion.63), kind=kCustom, calls=%fused_computation.clone | custom fusion | bytes 16781312 | tf_op jit(solution)/shard_map/jit(_take)/gather | solution.py:61
  167.3 16.8 %fusion.2 = bf16[1024,4,512]{2,1,0:T(4,128)(2,1)S(1)} fusion(f32[1024,4,512]{2,0,1:T(8,128)} %bitcast.41, f32[1024,4,512]{2,1,0:T(4,128)} %gather_fusion.1, f32[1024,4,512]{2,1,0:T(4,128)} %gather_fusion, pred[1024]{0:T(1024)(128)(4,1)S(1)} %get-tuple-element.15, pred[1024]{0:T(1024)(128)(4,1)S(1)} %get-tuple-element.16), kind=kLoop, calls=%fused_computation.7 | loop fusion | flops 10485760 | bytes 29362176 | tf_op jit(solution)/shard_map/convert_element_type | solution.py:63
  184.1 111.7 %all_to_all.33 = bf16[1024,4,512]{2,1,0:T(4,128)(2,1)S(1)} all-to-all(bf16[1024,4,512]{2,1,0:T(4,128)(2,1)S(1)} %fusion.2), channel_id=1, replica_groups=mesh['strip'=2,'ifg'=16] {'ifg'}, dimensions={0} | all-to-all | bytes 8388608 | tf_op jit(solution)/shard_map/all_to_all | solution.py:64
  295.8 0.8 copy.53
  296.6 0.5 copy.54
  297.1 0.0 copy-start.1
  297.1 4.4 %copy.56 = bf16[64,64,512]{2,1,0:T(8,128)(2,1)} copy(bf16[64,64,512]{2,0,1:T(8,128)(2,1)S(1)} %bitcast.44) | data formatting | bytes 8388608
  (10 shorter events, 0.1 us)
Async XLA Ops:
  0.6 18.6 %copy-start = (bf16[1024,1024]{1,0:T(8,128)(2,1)S(1)}, bf16[1024,1024]{1,0:T(8,128)(2,1)}, u32[]{:S(2)}) copy-start(bf16[1024,1024]{1,0:T(8,128)(2,1)} %param.10) | copy-start | bytes 6291460
  36.4 7.5 %copy-start.3 = (s32[1024,2]{0,1:T(2,128)S(1)}, s32[1024,2]{0,1:T(2,128)}, u32[]{:S(2)}) copy-start(s32[1024,2]{0,1:T(2,128)} %param.9) | copy-start | bytes 24580
  36.4 85.6 %all-to-all-start = ((bf16[64,64,512]{2,0,1:T(8,128)(2,1)}), bf16[64,64,512]{2,0,1:T(8,128)(2,1)}, u32[]{:S(2)}, u32[]{:S(2)}) async-start(bf16[64,64,512]{2,0,1:T(8,128)(2,1)} %copy.47), calls=%async_computation | async-start | bytes 8388608 | tf_op jit(solution)/shard_map/all_to_all | solution.py:56
  134.3 1.4 copy-start.4
  140.7 13.3 %copy-start.2 = (f32[256,4,512]{2,1,0:T(4,128)}, f32[256,4,512]{2,1,0:T(4,128)S(1)}, u32[]{:S(2)}) copy-start(f32[256,4,512]{2,1,0:T(4,128)S(1)} %copy.55) | copy-start | bytes 6291460
  297.1 4.4 %copy-start.1 = (bf16[1024,1024]{1,0:T(8,128)(2,1)S(1)}, bf16[1024,1024]{1,0:T(8,128)(2,1)}, u32[]{:S(2)}) copy-start(bf16[1024,1024]{1,0:T(8,128)(2,1)} %param.10) | copy-start | bytes 6291460
where the time goes:
time: 302 us
  blocking collectives  112 us (37%)
  waiting for transfers between devices  78 us (26%)
  local copies, waits for them, and re-layouts  54.8 us (18%)
  matrix products  31.1 us (10%)
  other arithmetic  17.6 us (6%)
  starting transfers between devices  7.48 us (2%)
    all_to_all x1, blocking collectives, per_device(): lax.all_to_all(residual_band, 'ifg', split_axis=0, concat_axis=1, tiled=T...  112 us
    all_to_all x1, waiting for transfers between devices, per_device(): lax.all_to_all(payload, 'ifg', split_axis=1, concat_axis=0, tiled=True)  78 us
    convert_element_type x1, other arithmetic, per_device(): (regrouped.astype(jnp.float32) - (later - earlier)).astype(jnp.bfloat16)  16.8 us
    dot_general x1, matrix products, per_device(): jnp.einsum('irc,cb->irb', masked, col_basis, precision=highest)  13.4 us
    gather x1, local copies, waits for them, and re-layouts, per_device(): earlier = jnp.take(displacement, date_pairs[:, 0], axis=0)  13.3 us
    gather x1, local copies, waits for them, and re-layouts, per_device(): later = jnp.take(displacement, date_pairs[:, 1], axis=0)  13.3 us
    dot_general x1, matrix products, evaluate_ramp(): return jnp.einsum('irb,cb->irc', ramp_rows, col_basis, precision=highest)  8.99 us
    unnamed x13, local copies, waits for them, and re-layouts  8.07 us
  transfers between devices with their start and end apart: 1, of which 1 were waited for; matrix products, arithmetic and copies ran while one was open for 0% of the time, Pallas kernels for 0%

commit v1 on v0

v1 whole, which is shorter than its diff:
```python
import functools

import jax
import jax.numpy as jnp
from jax import lax
from jax.experimental import pallas as pl
from jax.experimental.pallas import tpu as pltpu
from jax.sharding import PartitionSpec as P

KNOTS = 32
BLOCK = 16
PLANE = 4
LINE = 4
PARTS = 1

highest = lax.Precision.HIGHEST
f32 = jnp.float32
bf16 = jnp.bfloat16


def spline_basis(count, knot_count):
    spacing = (knot_count - 3) / (count - 1)
    places = jnp.arange(count, dtype=jnp.float32) * spacing
    centres = jnp.arange(knot_count, dtype=jnp.float32) - 1.0
    offset = jnp.abs(places[:, None] - centres[None, :])
    inner = 2.0 / 3.0 - offset * offset + 0.5 * offset**3
    outer = (2.0 - offset) ** 3 / 6.0
    return jnp.where(offset < 1.0, inner, jnp.where(offset < 2.0, outer, 0.0))


def weight_field(coherence):
    block_rows, block_cols = coherence.shape
    spread = jnp.broadcast_to(
        coherence.astype(jnp.float32)[:, None, :, None], (block_rows, BLOCK, block_cols, BLOCK)
    )
    return spread.reshape(block_rows * BLOCK, block_cols * BLOCK)


def fit_ramp(phases, coherence, ramp_inverse):
    local_count, row_count, col_count = phases.shape
    square = KNOTS * KNOTS
    row_basis = spline_basis(row_count, KNOTS)
    col_basis = spline_basis(col_count, KNOTS)
    masked = phases.astype(jnp.float32) * weight_field(coherence)
    partial_score = jnp.einsum("irc,cb->irb", masked, col_basis, precision=highest)
    score = jnp.einsum("ra,irb->iab", row_basis, partial_score, precision=highest)
    solved = jnp.dot(
        ramp_inverse.astype(jnp.float32), score.reshape(local_count, square).T, precision=highest
    )
    return solved.T.reshape(local_count, KNOTS, KNOTS), row_basis, col_basis


def per_device(phases, coherence, date_pairs, ramp_inverse, pseudo_inverse):
    row_count = phases.shape[1]
    row_share = row_count // lax.axis_size("ifg")
    coefficients, row_basis, col_basis = fit_ramp(phases, coherence, ramp_inverse)
    ramp_rows = jnp.einsum("ra,iab->irb", row_basis, coefficients, precision=highest)
    ramp = jnp.einsum("irb,cb->irc", ramp_rows, col_basis, precision=highest)
    payload = (phases.astype(jnp.float32) - ramp).astype(jnp.bfloat16)
    regrouped = lax.all_to_all(payload, "ifg", split_axis=1, concat_axis=0, tiled=True)
    total_count, _, col_count = regrouped.shape
    flat = regrouped.reshape(total_count, row_share * col_count)
    displacement = jnp.dot(pseudo_inverse, flat, preferred_element_type=jnp.float32)
    displacement = displacement.reshape(pseudo_inverse.shape[0], row_share, col_count)
    later = jnp.take(displacement, date_pairs[:, 1], axis=0)
    earlier = jnp.take(displacement, date_pairs[:, 0], axis=0)
    residual_band = (regrouped.astype(jnp.float32) - (later - earlier)).astype(jnp.bfloat16)
    residual_phase = lax.all_to_all(residual_band, "ifg", split_axis=0, concat_axis=1, tiled=True)
    return (displacement, residual_phase)


def line_kernel(
    corr, own_ref, out_ref, pair_ref, disp, resid,
    raw, near, far, mid_send, back_send, res_send,
    raw_ss, raw_rs, near_ss, near_rs, far_ss, far_rs, res_ss, res_rs,
):
    rows, count, cols = corr.shape
    chunks, total_count, width = raw.shape
    share = rows // (PLANE * LINE)
    me = lax.axis_index("ifg")
    z = me // PLANE
    q = me % PLANE
    side = z // 2
    inner_z = 1 + side
    outer_z = 3 * side
    is_inner = (z - outer_z) * (1 - 2 * side)
    beside = (inner_z + outer_z - z) * PLANE + q
    partner = (LINE - 1 - z) * PLANE + q
    MESH = pl.DeviceIdType.MESH

    def place(k, owner):
        row = k // PARTS
        return (row // share) * share * PLANE + owner * share + row % share, (k % PARTS) * width

    def peer(p):
        return (q + p) % PLANE

    def source(p):
        return (q + PLANE - p) % PLANE

    def raw_copy(k, p):
        row, col = place(k, peer(p))
        return pltpu.make_async_remote_copy(
            src_ref=corr.at[row, :, pl.ds(pl.multiple_of(col, width), width)],
            dst_ref=raw.at[k, pl.ds(pl.multiple_of(q * count, count), count), :],
            send_sem=raw_ss.at[k, p - 1], recv_sem=raw_rs.at[k, p - 1],
            device_id={"ifg": z * PLANE + peer(p)}, device_id_type=MESH)

    def res_copy(k, p):
        row, col = place(k, q)
        return pltpu.make_async_remote_copy(
            src_ref=res_send.at[k, pl.ds(pl.multiple_of(peer(p) * count, count), count), :],
            dst_ref=resid.at[row, :, pl.ds(pl.multiple_of(col, width), width)],
            send_sem=res_ss.at[k, p - 1], recv_sem=res_rs.at[k, p - 1],
            device_id={"ifg": z * PLANE + peer(p)}, device_id_type=MESH)

    def line_copy(src, dst, ss, rs, k, target):
        return pltpu.make_async_remote_copy(
            src_ref=src.at[k], dst_ref=dst.at[k], send_sem=ss.at[k], recv_sem=rs.at[k],
            device_id={"ifg": target}, device_id_type=MESH)

    barrier = pltpu.get_barrier_semaphore()
    for p in range(1, PLANE):
        pl.semaphore_signal(
            barrier, inc=1, device_id={"ifg": z * PLANE + peer(p)}, device_id_type=MESH)
    pl.semaphore_signal(barrier, inc=1, device_id={"ifg": beside}, device_id_type=MESH)

    @pl.when(is_inner == 1)
    def _():
        pl.semaphore_signal(barrier, inc=1, device_id={"ifg": partner}, device_id_type=MESH)

    pl.semaphore_wait(barrier, PLANE + is_inner)

    @pl.loop(0, chunks)
    def _(k):
        for p in range(1, PLANE):
            raw_copy(k, p).start()

    def dot(a, b):
        return jnp.dot(a, b, preferred_element_type=f32)

    def finish(k, total):
        row, col = place(k, q)

        @pl.when((k // PARTS) // share == z)
        def _():
            disp[(k // PARTS) % share, :, pl.ds(pl.multiple_of(col, width), width)] = total

        high = total.astype(bf16)
        low = (total - high.astype(f32)).astype(bf16)
        modeled = dot(pair_ref[...], high) + dot(pair_ref[...], low)
        res_send[k] = (raw[k].astype(f32) - modeled).astype(bf16)
        for p in range(1, PLANE):
            res_copy(k, p).start()
        resid[row, :, pl.ds(pl.multiple_of(col, width), width)] = res_send[
            k, pl.ds(pl.multiple_of(q * count, count), count), :]

    @pl.loop(0, chunks + 4)
    def _(t):
        @pl.when(t < chunks)
        def _():
            k = t
            row, col = place(k, q)
            raw[k, pl.ds(pl.multiple_of(q * count, count), count), :] = corr[
                row, :, pl.ds(pl.multiple_of(col, width), width)]
            for p in range(1, PLANE):
                raw_copy(k, p).wait_recv()

            @pl.when(is_inner == 0)
            def _():
                line_copy(raw, near, near_ss, near_rs, k, beside).start()

            @pl.when(is_inner == 1)
            def _():
                line_copy(raw, near, near_ss, near_rs, k, beside).wait_recv()
                half = dot(out_ref[...], near[k]) + dot(own_ref[...], raw[k])
                mid_send[k] = half.astype(bf16)
                line_copy(mid_send, far, far_ss.at[0], far_rs, k, partner).start()

        @pl.when((is_inner == 1) & (t >= 2) & (t < chunks + 2))
        def _():
            k = t - 2
            line_copy(mid_send, far, far_ss.at[0], far_rs, k, partner).wait_recv()
            rest = far[k].astype(f32) + dot(own_ref[...], raw[k])
            back_send[k] = rest.astype(bf16)
            line_copy(back_send, far, far_ss.at[1], far_rs, k, beside).start()
            finish(k, rest + dot(out_ref[...], near[k]))

        @pl.when((is_inner == 0) & (t >= 4))
        def _():
            k = t - 4
            line_copy(back_send, far, far_ss.at[1], far_rs, k, beside).wait_recv()
            finish(k, far[k].astype(f32) + dot(own_ref[...], raw[k]))

    @pl.loop(0, chunks)
    def _(k):
        for p in range(1, PLANE):
            raw_copy(k, p).wait_send()
            res_copy(k, p).wait_send()
            res_copy(k, p).wait_recv()

        @pl.when(is_inner == 0)
        def _():
            line_copy(raw, near, near_ss, near_rs, k, beside).wait_send()

        @pl.when(is_inner == 1)
        def _():
            line_copy(mid_send, far, far_ss.at[0], far_rs, k, partner).wait_send()
            line_copy(back_send, far, far_ss.at[1], far_rs, k, beside).wait_send()


def line_call(corrected, own, outer, pair):
    rows, count, cols = corrected.shape
    dates, total_count = own.shape
    chunks = rows // PLANE * PARTS
    width = cols // PARTS
    share = rows // (PLANE * LINE)
    slots = pltpu.VMEM((chunks, dates, width), bf16)
    sems = pltpu.SemaphoreType.DMA
    vmem = pl.BlockSpec(memory_space=pltpu.VMEM)
    return pl.pallas_call(
        line_kernel,
        out_shape=(
            jax.ShapeDtypeStruct((share, dates, cols), f32),
            jax.ShapeDtypeStruct((rows, count, cols), bf16),
        ),
        in_specs=[vmem] * 4,
        out_specs=(vmem, vmem),
        scratch_shapes=[slots] * 6 + [
            sems((chunks, PLANE - 1)), sems((chunks, PLANE - 1)),
            sems((chunks,)), sems((chunks,)),
            sems((2, chunks)), sems((chunks,)),
            sems((chunks, PLANE - 1)), sems((chunks, PLANE - 1)),
        ],
        compiler_params=pltpu.CompilerParams(
            collective_id=0, has_side_effects=True, vmem_limit_bytes=52 * 2**20),
        name="line_sums",
    )(corrected, own, outer, pair)


def per_device_line(phases, coherence, date_pairs, ramp_inverse, pseudo_inverse):
    dates, ifg_count = pseudo_inverse.shape
    plane_count = ifg_count // LINE
    z = lax.axis_index("ifg") // PLANE
    own = lax.dynamic_slice_in_dim(pseudo_inverse, z * plane_count, plane_count, 1)
    outer = lax.dynamic_slice_in_dim(pseudo_inverse, (z // 2) * 3 * plane_count, plane_count, 1)
    pairs = lax.dynamic_slice_in_dim(date_pairs, z * plane_count, plane_count, 0)
    numbers = jnp.arange(dates, dtype=jnp.int32)[None, :]
    pair = ((pairs[:, 1:] == numbers).astype(f32) - (pairs[:, :1] == numbers).astype(f32)).astype(bf16)
    coefficients, row_basis, col_basis = fit_ramp(phases, coherence, ramp_inverse)
    ramp_rows = jnp.einsum("ra,iab->rib", row_basis, coefficients, precision=highest)
    ramp = jnp.einsum("rib,cb->ric", ramp_rows, col_basis, precision=highest)
    corrected = (phases.transpose(1, 0, 2).astype(f32) - ramp).astype(bf16)
    displacement, residual = line_call(corrected, own, outer, pair)
    return displacement.transpose(1, 0, 2), residual.transpose(1, 0, 2)


def solution(mesh):
    placed = (P("ifg", "strip", None), P("strip", None), P(), P(), P())
    on_line = mesh.shape["ifg"] == PLANE * LINE

    def run(phases, coherence, date_pairs, ramp_inverse, pseudo_inverse):
        dates, ifg_count = pseudo_inverse.shape
        fits = on_line and dates == ifg_count // LINE
        return jax.shard_map(
            per_device_line if fits else per_device,
            mesh=mesh,
            in_specs=placed,
            out_specs=(P(None, ("strip", "ifg"), None), P("ifg", "strip", None)),
            check_vma=False,
        )(phases, coherence, date_pairs, ramp_inverse, pseudo_inverse)

    return run
```

time: 302 us -> 182 us (0.60)
  Pallas kernels: 0 us -> 130 us
  blocking collectives: 112 us -> 0 us
  waiting for transfers between devices: 78 us -> 0 us
  local copies, waits for them, and re-layouts: 54.8 us -> 14 us
  other arithmetic: 17.6 us -> 0.84 us
  starting transfers between devices: 7.48 us -> 0 us
  matrix products: 31.1 us -> 35.7 us
    pallas_call x0 -> x1, Pallas kernels: none -> 130 us  [line_call(): pl.pallas_call(line_kernel, out_shape=(jax.ShapeDtypeStruct((share, dates...]
    all_to_all x1 -> x0, blocking collectives: 112 us -> none  [per_device(): lax.all_to_all(residual_band, 'ifg', split_axis=0, concat_axis=1, tiled=T...]
    all_to_all x1 -> x0, waiting for transfers between devices: 78 us -> none  [per_device(): lax.all_to_all(payload, 'ifg', split_axis=1, concat_axis=0, tiled=True)]
    gather x2 -> x0, local copies, waits for them, and re-layouts: 26.6 us -> none  [the longest x1 13.3 us: per_device(): earlier = jnp.take(displacement, date_pairs[:, 0], axis=0)]
    convert_element_type x1, other arithmetic: 16.8 us -> 0.13 us  [per_device_line(): ((pairs[:, 1:] == numbers).astype(f32) - (pairs[:, :1] == numbers).astype...]
    convert_element_type x2 -> x0, local copies, waits for them, and re-layouts: 11 us -> none  [the longest x1 6.61 us: per_device(): regrouped.astype(jnp.float32) - (later - earlier)]
    all_to_all x1 -> x0, starting transfers between devices: 7.48 us -> none  [per_device(): lax.all_to_all(payload, 'ifg', split_axis=1, concat_axis=0, tiled=True)]
    all_to_all x3 -> x0, local copies, waits for them, and re-layouts: 7.04 us -> none  [the longest x1 5.72 us: per_device(): lax.all_to_all(payload, 'ifg', split_axis=1, concat_axis=0, tiled=True)]
  transfers between devices with their start and end apart: 1 -> 0, of which waited for: 1 -> 0; matrix products, arithmetic and copies ran while one was open for 0% -> 0% of each run, Pallas kernels for 0% -> 0%
where the time goes in v1:
time: 182 us
  Pallas kernels  130 us (71%)
  matrix products  35.7 us (20%)
  local copies, waits for them, and re-layouts  14 us (8%)
    pallas_call x1, Pallas kernels, line_call(): pl.pallas_call(line_kernel, out_shape=(jax.ShapeDtypeStruct((share, dates...  130 us
    dot_general x1, matrix products, fit_ramp(): jnp.einsum('irc,cb->irb', masked, col_basis, precision=highest)  17.6 us
    dot_general x1, matrix products, per_device_line(): ramp = jnp.einsum('rib,cb->ric', ramp_rows, col_basis, precision=highest)  13.7 us
    unnamed x8, local copies, waits for them, and re-layouts  10.4 us

profile of v1, /device:TPU:1, one launch (start us, length us, event | category | flops | bytes accessed | tf_op | source)
XLA Modules:
  0.0 181.7 jit_solution(3403875382076223588)
XLA Ops:
  0.6 0.0 copy-start
  0.7 1.5 copy-done
  2.2 0.8 fusion.91
  3.1 0.7 convert_element_type.28
  3.8 0.1 subtract_convert_fusion.pair_ref
  3.9 1.0 constant_dynamic-slice_fusion.1
  4.9 0.2 broadcast_in_dim.11
  5.1 1.3 mul.73
  6.4 17.6 %fusion.2 = f32[64,64,32]{0,2,1:T(8,128)S(1)} fusion(f32[64,512]{1,0:T(8,128)} %mul.73, bf16[64,64,512]{2,1,0:T(8,128)(2,1)} %param.5, f32[32]{0:T(128)S(1)} %iota_add_fusion, f32[512]{0:T(512)S(1)} %iota_multiply_fusion), kind=kOutput, calls=%fused_computation.4 | convolution fusion | flops 809746432 | bytes 4851840 | tf_op jit(solution)/shard_map/irc,cb->irb/dot_general | solution.py:45
  24.0 1.3 convolution_bitcast_fusion
  25.3 0.0 copy-start.2
  25.3 0.3 copy.11
  25.6 1.8 %fusion.92 = f32[64,32,32]{0,2,1:T(8,128)S(1)} fusion(f32[64,1024,1]{0,1,2:T(8,128)S(1)} %bitcast.31, bf16[32,32,1024]{2,1,0:T(8,128)(2,1)S(1)} %bitcast.28), kind=kOutput, calls=%fused_computation.106 | convolution fusion | flops 805306368 | bytes 2621440 | tf_op jit(solution)/shard_map/dot_general | solution.py:47
  27.5 1.3 fusion.7
  28.8 0.0 copy-done.2
  28.8 13.7 %fusion.1.corr = bf16[64,64,512]{2,1,0:T(8,128)(2,1)} fusion(bf16[64,64,512]{2,1,0:T(8,128)(2,1)S(1)} %copy-done.2, f32[64,64,32]{1,0,2:T(8,128)S(1)} %fusion.7, f32[32]{0:T(128)S(1)} %iota_add_fusion, f32[512]{0:T(512)S(1)} %iota_multiply_fusion), kind=kOutput, calls=%fused_computation.3 | convolution fusion | flops 811843584 | bytes 8915072 | tf_op jit(solution)/shard_map/rib,cb->ric/dot_general | solution.py:252
  42.5 130.4 %line_sums.1 = (f32[4,256,512]{2,1,0:T(8,128)}, bf16[64,64,512]{2,1,0:T(8,128)(2,1)}) custom-call(bf16[64,64,512]{2,1,0:T(8,128)(2,1)} %fusion.1.corr, bf16[256,256]{1,0:T(8,128)(2,1)S(1)} %get-tuple-element.11.own_ref, bf16[256,256]{1,0:T(8,128)(2,1)S(1)} %get-tuple-element.10.out_ref, bf16[256,256]{1,0:T(8,128)(2,1)S(1)} %subtract_convert_fusion.pair_ref), custom_call_target="tpu_custom_call" | custom-call | tf_op jit(solution)/shard_map/line_sums/pallas_call | solution.py:221
  172.9 0.0 copy-start.1
  172.9 4.4 %copy.12 = f32[256,4,512]{2,1,0:T(4,128)} copy(f32[256,4,512]{2,0,1:T(8,128)} %bitcast.30) | data formatting | bytes 4194304
  177.3 0.0 copy-done.1
  177.3 4.4 %copy.13 = bf16[64,64,512]{2,1,0:T(8,128)(2,1)} copy(bf16[64,64,512]{2,0,1:T(8,128)(2,1)S(1)} %bitcast.29) | data formatting | bytes 8388608
  (3 shorter events, 0.0 us)
Async XLA Ops:
  0.6 1.6 copy-start
  25.3 3.5 %copy-start.2 = (bf16[64,64,512]{2,1,0:T(8,128)(2,1)S(1)}, bf16[64,64,512]{2,1,0:T(8,128)(2,1)}, u32[]{:S(2)}) copy-start(bf16[64,64,512]{2,1,0:T(8,128)(2,1)} %param.5) | copy-start | bytes 12582916
  172.9 4.4 %copy-start.1 = (bf16[64,64,512]{2,1,0:T(8,128)(2,1)S(1)}, bf16[64,64,512]{2,1,0:T(8,128)(2,1)}, u32[]{:S(2)}) copy-start(bf16[64,64,512]{2,1,0:T(8,128)(2,1)} %get-tuple-element.5) | copy-start | bytes 12582916

commit v2 on v1

--- a/solution.py
+++ b/solution.py
@@ -12,6 +12,8 @@
 PLANE = 4
 LINE = 4
 PARTS = 1
+LEAD = 3
+SKEW = 2
 
 highest = lax.Precision.HIGHEST
 f32 = jnp.float32
@@ -70,11 +72,11 @@
 
 
 def line_kernel(
-    corr, own_ref, out_ref, pair_ref, disp, resid,
-    raw, near, far, mid_send, back_send, res_send,
+    phase_ref, ramp_ref, basis_ref, own_ref, out_ref, pair_ref, disp, resid,
+    corr, raw, near, far, mid_send, back_send, res_send,
     raw_ss, raw_rs, near_ss, near_rs, far_ss, far_rs, res_ss, res_rs,
 ):
-    rows, count, cols = corr.shape
+    rows, count, cols = phase_ref.shape
     chunks, total_count, width = raw.shape
     share = rows // (PLANE * LINE)
     me = lax.axis_index("ifg")
@@ -95,13 +97,9 @@
     def peer(p):
         return (q + p) % PLANE
 
-    def source(p):
-        return (q + PLANE - p) % PLANE
-
     def raw_copy(k, p):
-        row, col = place(k, peer(p))
         return pltpu.make_async_remote_copy(
-            src_ref=corr.at[row, :, pl.ds(pl.multiple_of(col, width), width)],
+            src_ref=corr.at[k, p - 1],
             dst_ref=raw.at[k, pl.ds(pl.multiple_of(q * count, count), count), :],
             send_sem=raw_ss.at[k, p - 1], recv_sem=raw_rs.at[k, p - 1],
             device_id={"ifg": z * PLANE + peer(p)}, device_id_type=MESH)
@@ -131,13 +129,24 @@
 
     pl.semaphore_wait(barrier, PLANE + is_inner)
 
-    @pl.loop(0, chunks)
-    def _(k):
-        for p in range(1, PLANE):
-            raw_copy(k, p).start()
-
     def dot(a, b):
         return jnp.dot(a, b, preferred_element_type=f32)
+
+    def produce(k):
+        for p in range(1, PLANE + 1):
+            row, col = place(k, peer(p))
+            part = pl.ds(pl.multiple_of(col, width), width)
+            ramp = dot(ramp_ref[row], basis_ref[:, part])
+            corrected = (phase_ref[row, :, part].astype(f32) - ramp).astype(bf16)
+            if p == PLANE:
+                raw[k, pl.ds(pl.multiple_of(q * count, count), count), :] = corrected
+            else:
+                corr[k, p - 1] = corrected
+                raw_copy(k, p).start()
+
+    @pl.loop(0, LEAD)
+    def _(k):
+        produce(k)
 
     def finish(k, total):
         row, col = place(k, q)
@@ -155,14 +164,15 @@
         resid[row, :, pl.ds(pl.multiple_of(col, width), width)] = res_send[
             k, pl.ds(pl.multiple_of(q * count, count), count), :]
 
-    @pl.loop(0, chunks + 4)
+    @pl.loop(0, chunks + 2 * SKEW)
     def _(t):
+        @pl.when(t + LEAD < chunks)
+        def _():
+            produce(t + LEAD)
+
         @pl.when(t < chunks)
         def _():
             k = t
-            row, col = place(k, q)
-            raw[k, pl.ds(pl.multiple_of(q * count, count), count), :] = corr[
-                row, :, pl.ds(pl.multiple_of(col, width), width)]
             for p in range(1, PLANE):
                 raw_copy(k, p).wait_recv()
 
@@ -177,18 +187,18 @@
                 mid_send[k] = half.astype(bf16)
                 line_copy(mid_send, far, far_ss.at[0], far_rs, k, partner).start()
 
-        @pl.when((is_inner == 1) & (t >= 2) & (t < chunks + 2))
-        def _():
-            k = t - 2
+        @pl.when((is_inner == 1) & (t >= SKEW) & (t < chunks + SKEW))
+        def _():
+            k = t - SKEW
             line_copy(mid_send, far, far_ss.at[0], far_rs, k, partner).wait_recv()
             rest = far[k].astype(f32) + dot(own_ref[...], raw[k])
             back_send[k] = rest.astype(bf16)
             line_copy(back_send, far, far_ss.at[1], far_rs, k, beside).start()
             finish(k, rest + dot(out_ref[...], near[k]))
 
-        @pl.when((is_inner == 0) & (t >= 4))
-        def _():
-            k = t - 4
+        @pl.when((is_inner == 0) & (t >= 2 * SKEW))
+        def _():
+            k = t - 2 * SKEW
             line_copy(back_send, far, far_ss.at[1], far_rs, k, beside).wait_recv()
             finish(k, far[k].astype(f32) + dot(own_ref[...], raw[k]))
 
@@ -209,8 +219,8 @@
             line_copy(back_send, far, far_ss.at[1], far_rs, k, beside).wait_send()
 
 
-def line_call(corrected, own, outer, pair):
-    rows, count, cols = corrected.shape
+def line_call(phases, ramp_rows, basis, own, outer, pair):
+    rows, count, cols = phases.shape
     dates, total_count = own.shape
     chunks = rows // PLANE * PARTS
     width = cols // PARTS
@@ -224,9 +234,9 @@
             jax.ShapeDtypeStruct((share, dates, cols), f32),
             jax.ShapeDtypeStruct((rows, count, cols), bf16),
         ),
-        in_specs=[vmem] * 4,
+        in_specs=[vmem] * 6,
         out_specs=(vmem, vmem),
-        scratch_shapes=[slots] * 6 + [
+        scratch_shapes=[pltpu.VMEM((chunks, PLANE - 1, count, width), bf16)] + [slots] * 6 + [
             sems((chunks, PLANE - 1)), sems((chunks, PLANE - 1)),
             sems((chunks,)), sems((chunks,)),
             sems((2, chunks)), sems((chunks,)),
@@ -235,7 +245,12 @@
         compiler_params=pltpu.CompilerParams(
             collective_id=0, has_side_effects=True, vmem_limit_bytes=52 * 2**20),
         name="line_sums",
-    )(corrected, own, outer, pair)
+    )(phases, ramp_rows, basis, own, outer, pair)
+
+
+def split(values):
+    high = values.astype(bf16)
+    return high, (values - high.astype(f32)).astype(bf16)
 
 
 def per_device_line(phases, coherence, date_pairs, ramp_inverse, pseudo_inverse):
@@ -247,11 +262,25 @@
     pairs = lax.dynamic_slice_in_dim(date_pairs, z * plane_count, plane_count, 0)
     numbers = jnp.arange(dates, dtype=jnp.int32)[None, :]
     pair = ((pairs[:, 1:] == numbers).astype(f32) - (pairs[:, :1] == numbers).astype(f32)).astype(bf16)
-    coefficients, row_basis, col_basis = fit_ramp(phases, coherence, ramp_inverse)
+    local_count, row_count, col_count = phases.shape
+    row_basis = spline_basis(row_count, KNOTS)
+    col_basis = spline_basis(col_count, KNOTS)
+    high, low = split(col_basis)
+    masked = jnp.where(weight_field(coherence) > 0, phases, jnp.zeros_like(phases))
+    halves = jnp.einsum(
+        "irc,cb->irb", masked, jnp.concatenate([high, low], 1), preferred_element_type=f32)
+    partial_score = halves[:, :, :KNOTS] + halves[:, :, KNOTS:]
+    score = jnp.einsum("ra,irb->iab", row_basis, partial_score, precision=highest)
+    coefficients = jnp.dot(
+        ramp_inverse.astype(f32), score.reshape(local_count, -1).T, precision=highest
+    ).T.reshape(local_count, KNOTS, KNOTS)
     ramp_rows = jnp.einsum("ra,iab->rib", row_basis, coefficients, precision=highest)
-    ramp = jnp.einsum("rib,cb->ric", ramp_rows, col_basis, precision=highest)
-    corrected = (phases.transpose(1, 0, 2).astype(f32) - ramp).astype(bf16)
-    displacement, residual = line_call(corrected, own, outer, pair)
+    rows_high, rows_low = split(ramp_rows)
+    displacement, residual = line_call(
+        phases.transpose(1, 0, 2),
+        jnp.concatenate([rows_high, rows_high, rows_low], 2),
+        jnp.concatenate([high, low, high], 1).T,
+        own, outer, pair)
     return displacement.transpose(1, 0, 2), residual.transpose(1, 0, 2)
 
 

time: 182 us -> 171 us (0.940)
  matrix products: 35.7 us -> 11.3 us
  local copies, waits for them, and re-layouts: 14 us -> 24.2 us
  other arithmetic: 0.84 us -> 4.48 us
    dot_general x4 -> x3, matrix products: 34.4 us -> 10.2 us  [the longest x1 4.3 us: per_device_line(): jnp.einsum('irc,cb->irb', masked, jnp.concatenate([high, low], 1), prefer...]
    unnamed x8 -> x13, local copies, waits for them, and re-layouts: 10.4 us -> 16 us
    dot_general x0 -> x2, local copies, waits for them, and re-layouts: none -> 3.79 us  [per_device_line(): jnp.einsum('ra,iab->rib', row_basis, coefficients, precision=highest)]
where the time goes in v2:
time: 171 us
  Pallas kernels  130 us (76%)
  local copies, waits for them, and re-layouts  24.2 us (14%)
  matrix products  11.3 us (7%)
  other arithmetic  4.48 us (3%)
    pallas_call x1, Pallas kernels, line_call(): pl.pallas_call(line_kernel, out_shape=(jax.ShapeDtypeStruct((share, dates...  130 us
    unnamed x13, local copies, waits for them, and re-layouts  16 us
    dot_general x1, matrix products, per_device_line(): jnp.einsum('irc,cb->irb', masked, jnp.concatenate([high, low], 1), prefer...  4.3 us
    dot_general x2, local copies, waits for them, and re-layouts, per_device_line(): jnp.einsum('ra,iab->rib', row_basis, coefficients, precision=highest)  3.79 us

profile of v2, /device:TPU:1, one launch (start us, length us, event | category | flops | bytes accessed | tf_op | source)
XLA Modules:
  0.0 170.9 jit_solution(14078484277041052607)
XLA Ops:
  0.6 0.0 copy-start
  0.7 1.5 copy-done
  2.2 0.7 convert_compare_fusion
  2.9 0.8 fusion.64
  3.8 0.1 fusion.19
  3.9 0.1 subtract_convert_fusion.1.pair_ref
  4.0 1.0 constant_dynamic-slice_fusion.1
  5.0 0.1 broadcast_in_dim.27
  5.2 0.8 gt.12
  6.0 4.3 %fusion = f32[64,64,64]{1,2,0:T(8,128)S(1)} fusion(bf16[64,64,512]{2,1,0:T(8,128)(2,1)} %param.5, pred[64,512]{1,0:T(8,128)(4,1)S(1)} %gt.12, bf16[512,32]{0,1:T(8,128)(2,1)S(1)} %get-tuple-element.17, bf16[512,32]{0,1:T(8,128)(2,1)S(1)} %get-tuple-element.16), kind=kOutput, calls=%fused_computation.1 | convolution fusion | flops 270663680 | bytes 5341184 | tf_op jit(solution)/shard_map/irc,cb->irb/dot_general | solution.py:270
  10.3 0.2 slice_add_fusion
  10.5 3.1 %convolution_bitcast_fusion = f32[64,32,32]{0,1,2:T(8,128)S(1)} fusion(f32[64,64,32]{1,2,0:T(8,128)S(1)} %slice_add_fusion, f32[32]{0:T(128)S(1)} %iota_add_fusion, f32[64]{0:T(128)S(1)} %iota_multiply_fusion.1), kind=kOutput, calls=%fused_computation.8 | convolution fusion | flops 50362368 | bytes 786816 | tf_op jit(solution)/shard_map/ra,irb->iab/dot_general | solution.py:273
  13.6 0.3 copy.22
  13.9 2.8 %fusion.3 = f32[64,32,32]{0,1,2:T(8,128)S(1)} fusion(f32[64,1024,1]{0,1,2:T(8,128)S(1)} %bitcast.30, bf16[32,32,1024]{2,1,0:T(8,128)(2,1)S(1)} %bitcast.26), kind=kOutput, calls=%fused_computation.4 | convolution fusion | flops 805306368 | bytes 2621440 | tf_op jit(solution)/shard_map/dot_general | solution.py:274
  16.7 1.1 fusion.31
  17.8 0.0 copy-start.1
  17.8 1.0 copy-done.1
  18.8 0.6 copy.40
  19.4 1.3 copy.28
  20.7 3.2 %copy.27 = f32[64,64,32]{2,1,0:T(8,128)} copy(f32[64,64,32]{1,0,2:T(8,128)} %copy-done.1) | data formatting | bytes 1048576 | tf_op jit(solution)/shard_map/ra,iab->rib/dot_general | solution.py:277
  23.9 0.0 copy-start.2
  23.9 0.0 copy-start.3
  23.9 2.3 %subtract_convert_fusion = bf16[64,64,32]{2,1,0:T(8,128)(2,1)S(1)} fusion(f32[64,64,32]{2,1,0:T(8,128)} %copy.27, bf16[64,64,32]{2,1,0:T(8,128)(2,1)} %copy.28), kind=kLoop, calls=%fused_computation.6 | loop fusion | flops 393216 | bytes 1048576 | tf_op jit(solution)/shard_map/convert_element_type | solution.py:253
  26.3 0.0 copy-done.2
  26.3 1.0 pad_maximum_fusion.ramp_ref
  27.2 0.1 copy-done.3
  27.4 4.5 %copy.41 = bf16[64,64,512]{2,0,1:T(8,128)(2,1)} copy(bf16[64,64,512]{2,1,0:T(8,128)(2,1)S(1)} %copy-done.3) | data formatting | bytes 8388608 | tf_op args[0]
  31.9 130.2 %line_sums.1 = (f32[4,256,512]{2,1,0:T(8,128)}, bf16[64,64,512]{2,1,0:T(8,128)(2,1)}) custom-call(bf16[64,64,512]{2,1,0:T(8,128)(2,1)} %bitcast.27, bf16[64,64,96]{2,1,0:T(8,128)(2,1)S(1)} %pad_maximum_fusion.ramp_ref, bf16[96,512]{1,0:T(8,128)(2,1)S(1)} %maximum_bitcast_fusion.basis_ref, bf16[256,256]{1,0:T(8,128)(2,1)S(1)} %get-tuple-element.13.own_ref, ...), custom_call_target="tpu_custom_call" | custom-call | tf_op jit(solution)/shard_map/line_sums/pallas_call | solution.py:231
  162.1 0.0 copy-start.4
  162.1 4.4 %copy.30 = f32[256,4,512]{2,1,0:T(4,128)} copy(f32[256,4,512]{2,0,1:T(8,128)} %bitcast.29) | data formatting | bytes 4194304
  166.5 0.0 copy-done.4
  166.5 4.4 %copy.31 = bf16[64,64,512]{2,1,0:T(8,128)(2,1)} copy(bf16[64,64,512]{2,0,1:T(8,128)(2,1)S(1)} %bitcast.28) | data formatting | bytes 8388608
  (4 shorter events, 0.0 us)
Async XLA Ops:
  0.6 1.6 copy-start
  17.8 1.0 copy-start.1
  23.9 2.4 %copy-start.2 = (bf16[64,64,32]{2,1,0:T(8,128)(2,1)S(1)}, bf16[64,64,32]{2,1,0:T(8,128)(2,1)}, u32[]{:S(2)}) copy-start(bf16[64,64,32]{2,1,0:T(8,128)(2,1)} %copy.28) | copy-start | bytes 786436
  23.9 3.5 %copy-start.3 = (bf16[64,64,512]{2,1,0:T(8,128)(2,1)S(1)}, bf16[64,64,512]{2,1,0:T(8,128)(2,1)}, u32[]{:S(2)}) copy-start(bf16[64,64,512]{2,1,0:T(8,128)(2,1)} %param.5) | copy-start | bytes 12582916
  162.1 4.4 %copy-start.4 = (bf16[64,64,512]{2,1,0:T(8,128)(2,1)S(1)}, bf16[64,64,512]{2,1,0:T(8,128)(2,1)}, u32[]{:S(2)}) copy-start(bf16[64,64,512]{2,1,0:T(8,128)(2,1)} %get-tuple-element.5) | copy-start | bytes 12582916

commit v3 on v2

--- a/solution.py
+++ b/solution.py
@@ -11,9 +11,9 @@
 BLOCK = 16
 PLANE = 4
 LINE = 4
-PARTS = 1
-LEAD = 3
-SKEW = 2
+PARTS = 2
+LEAD = 4
+SKEW = 3
 
 highest = lax.Precision.HIGHEST
 f32 = jnp.float32
@@ -73,7 +73,7 @@
 
 def line_kernel(
     phase_ref, ramp_ref, basis_ref, own_ref, out_ref, pair_ref, disp, resid,
-    corr, raw, near, far, mid_send, back_send, res_send,
+    corr, own_part, out_part, raw, near, far, mid_send, back_send, res_send,
     raw_ss, raw_rs, near_ss, near_rs, far_ss, far_rs, res_ss, res_rs,
 ):
     rows, count, cols = phase_ref.shape
@@ -183,18 +183,23 @@
             @pl.when(is_inner == 1)
             def _():
                 line_copy(raw, near, near_ss, near_rs, k, beside).wait_recv()
-                half = dot(out_ref[...], near[k]) + dot(own_ref[...], raw[k])
-                mid_send[k] = half.astype(bf16)
+                slot = k % (SKEW + 1)
+                own_sum = dot(own_ref[...], raw[k])
+                out_sum = dot(out_ref[...], near[k])
+                own_part[slot] = own_sum
+                out_part[slot] = out_sum
+                mid_send[k] = (own_sum + out_sum).astype(bf16)
                 line_copy(mid_send, far, far_ss.at[0], far_rs, k, partner).start()
 
         @pl.when((is_inner == 1) & (t >= SKEW) & (t < chunks + SKEW))
         def _():
             k = t - SKEW
             line_copy(mid_send, far, far_ss.at[0], far_rs, k, partner).wait_recv()
-            rest = far[k].astype(f32) + dot(own_ref[...], raw[k])
+            slot = k % (SKEW + 1)
+            rest = far[k].astype(f32) + own_part[slot]
             back_send[k] = rest.astype(bf16)
             line_copy(back_send, far, far_ss.at[1], far_rs, k, beside).start()
-            finish(k, rest + dot(out_ref[...], near[k]))
+            finish(k, rest + out_part[slot])
 
         @pl.when((is_inner == 0) & (t >= 2 * SKEW))
         def _():
@@ -236,7 +241,7 @@
         ),
         in_specs=[vmem] * 6,
         out_specs=(vmem, vmem),
-        scratch_shapes=[pltpu.VMEM((chunks, PLANE - 1, count, width), bf16)] + [slots] * 6 + [
+        scratch_shapes=[pltpu.VMEM((chunks, PLANE - 1, count, width), bf16)] + [pltpu.VMEM((SKEW + 1, dates, width), f32)] * 2 + [slots] * 6 + [
             sems((chunks, PLANE - 1)), sems((chunks, PLANE - 1)),
             sems((chunks,)), sems((chunks,)),
             sems((2, chunks)), sems((chunks,)),
@@ -248,9 +253,74 @@
     )(phases, ramp_rows, basis, own, outer, pair)
 
 
+def ramp_kernel(
+    phase_ref, weight_ref, basis_ref, inverse_ref, row_ref, rows_out, score, flat, coef,
+):
+    rows, count, cols = phase_ref.shape
+    group = 4
+
+    def first(r):
+        return jnp.minimum((r * (KNOTS - 3)) // (rows - 1), KNOTS - 4)
+
+    score[...] = jnp.zeros_like(score)
+
+    @pl.loop(0, rows // group)
+    def _(g):
+        r0 = g * group
+        masked = phase_ref[pl.ds(r0, group)] * weight_ref[pl.ds(r0, group)]
+        both = jnp.dot(
+            masked.reshape(group * count, cols), basis_ref[...], preferred_element_type=f32)
+        part = both[:, :KNOTS] + both[:, KNOTS:]
+        for j in range(group):
+            base = first(r0 + j)
+            for d in range(4):
+                score[base + d] += row_ref[r0 + j, base + d] * part[j * count:(j + 1) * count]
+
+    for a in range(KNOTS):
+        flat[:, a * KNOTS:(a + 1) * KNOTS] = score[a]
+    high = flat[...].astype(bf16)
+    low = (flat[...] - high.astype(f32)).astype(bf16)
+    across = (((1,), (1,)), ((), ()))
+    flat[...] = lax.dot_general(
+        high, inverse_ref[...], across, preferred_element_type=f32
+    ) + lax.dot_general(low, inverse_ref[...], across, preferred_element_type=f32)
+    for a in range(KNOTS):
+        coef[a] = flat[:, a * KNOTS:(a + 1) * KNOTS]
+
+    @pl.loop(0, rows // group)
+    def _(g):
+        for j in range(group):
+            r = g * group + j
+            base = first(r)
+            line = row_ref[r, base] * coef[base]
+            for d in range(1, 4):
+                line += row_ref[r, base + d] * coef[base + d]
+            top = line.astype(bf16)
+            rest = (line - top.astype(f32)).astype(bf16)
+            rows_out[r] = jnp.concatenate([top, top, rest], 1)
+
+
+def ramp_call(by_row, weight, basis, ramp_inverse, row_basis):
+    rows, count, cols = by_row.shape
+    vmem = pl.BlockSpec(memory_space=pltpu.VMEM)
+    return pl.pallas_call(
+        ramp_kernel,
+        out_shape=jax.ShapeDtypeStruct((rows, count, 3 * KNOTS), bf16),
+        in_specs=[vmem] * 4 + [pl.BlockSpec(memory_space=pltpu.SMEM)],
+        out_specs=vmem,
+        scratch_shapes=[
+            pltpu.VMEM((KNOTS, count, KNOTS), f32),
+            pltpu.VMEM((count, KNOTS * KNOTS), f32),
+            pltpu.VMEM((KNOTS, count, KNOTS), f32),
+        ],
+        compiler_params=pltpu.CompilerParams(vmem_limit_bytes=32 * 2**20),
+        name="ramp_fit",
+    )(by_row, weight, basis, ramp_inverse, row_basis)
+
+
 def split(values):
-    high = values.astype(bf16)
-    return high, (values - high.astype(f32)).astype(bf16)
+    high = lax.reduce_precision(values, exponent_bits=8, mantissa_bits=7)
+    return high.astype(bf16), (values - high).astype(bf16)
 
 
 def per_device_line(phases, coherence, date_pairs, ramp_inverse, pseudo_inverse):
@@ -264,21 +334,14 @@
     pair = ((pairs[:, 1:] == numbers).astype(f32) - (pairs[:, :1] == numbers).astype(f32)).astype(bf16)
     local_count, row_count, col_count = phases.shape
     row_basis = spline_basis(row_count, KNOTS)
-    col_basis = spline_basis(col_count, KNOTS)
-    high, low = split(col_basis)
-    masked = jnp.where(weight_field(coherence) > 0, phases, jnp.zeros_like(phases))
-    halves = jnp.einsum(
-        "irc,cb->irb", masked, jnp.concatenate([high, low], 1), preferred_element_type=f32)
-    partial_score = halves[:, :, :KNOTS] + halves[:, :, KNOTS:]
-    score = jnp.einsum("ra,irb->iab", row_basis, partial_score, precision=highest)
-    coefficients = jnp.dot(
-        ramp_inverse.astype(f32), score.reshape(local_count, -1).T, precision=highest
-    ).T.reshape(local_count, KNOTS, KNOTS)
-    ramp_rows = jnp.einsum("ra,iab->rib", row_basis, coefficients, precision=highest)
-    rows_high, rows_low = split(ramp_rows)
+    high, low = split(spline_basis(col_count, KNOTS))
+    by_row = phases.transpose(1, 0, 2)
+    ramp_rows = ramp_call(
+        by_row,
+        weight_field(coherence).astype(bf16).reshape(row_count, 1, col_count),
+        jnp.concatenate([high, low], 1), ramp_inverse, row_basis)
     displacement, residual = line_call(
-        phases.transpose(1, 0, 2),
-        jnp.concatenate([rows_high, rows_high, rows_low], 2),
+        by_row, ramp_rows,
         jnp.concatenate([high, low, high], 1).T,
         own, outer, pair)
     return displacement.transpose(1, 0, 2), residual.transpose(1, 0, 2)

time: 171 us -> 153 us (0.89)
  matrix products: 11.3 us -> 0 us
  local copies, waits for them, and re-layouts: 24.2 us -> 16 us
  Pallas kernels: 130 us -> 135 us
  other arithmetic: 4.48 us -> 1.06 us
    dot_general x4 -> x0, matrix products: 11.3 us -> none  [the longest x1 4.3 us: per_device_line(): jnp.einsum('irc,cb->irb', masked, jnp.concatenate([high, low], 1), prefer...]
    pallas_call x0 -> x1, Pallas kernels: none -> 9.77 us  [ramp_call(): pl.pallas_call(ramp_kernel, out_shape=jax.ShapeDtypeStruct((rows, count,...]
    pallas_call x1, Pallas kernels: 130 us -> 125 us  [line_call(): pl.pallas_call(line_kernel, out_shape=(jax.ShapeDtypeStruct((share, dates...]
    dot_general x2 -> x0, local copies, waits for them, and re-layouts: 3.79 us -> none  [per_device_line(): jnp.einsum('ra,iab->rib', row_basis, coefficients, precision=highest)]
    unnamed x13 -> x9, local copies, waits for them, and re-layouts: 16 us -> 13.5 us
where the time goes in v3:
time: 153 us; the launch traced here: 152 us
  Pallas kernels  135 us (88%)
  local copies, waits for them, and re-layouts  16 us (10%)
    pallas_call x1, Pallas kernels, line_call(): pl.pallas_call(line_kernel, out_shape=(jax.ShapeDtypeStruct((share, dates...  125 us
    unnamed x9, local copies, waits for them, and re-layouts  13.5 us
    pallas_call x1, Pallas kernels, ramp_call(): pl.pallas_call(ramp_kernel, out_shape=jax.ShapeDtypeStruct((rows, count,...  9.77 us

profile of v3, /device:TPU:1, one launch (start us, length us, event | category | flops | bytes accessed | tf_op | source)
XLA Modules:
  0.0 152.4 jit_solution(17931264126191793215)
XLA Ops:
  0.7 0.7 convert_convert_fusion
  1.4 0.8 fusion.21
  2.2 0.1 fusion.17.row_ref
  2.3 0.1 reduce-precision_convert_fusion
  2.5 0.1 copy.13.basis_ref
  2.6 0.1 subtract_convert_fusion.pair_ref
  2.7 1.0 constant_dynamic-slice_fusion.1
  3.8 0.1 broadcast_in_dim.10
  3.9 0.3 convert_element_type.46.weight_ref
  4.2 0.0 copy-start.1
  4.3 4.7 %copy.17 = bf16[64,64,512]{2,0,1:T(8,128)(2,1)S(1)} copy(bf16[64,64,512]{2,1,0:T(8,128)(2,1)} %param.5) | data formatting | bytes 8388608 | tf_op args[0]
  8.9 0.0 copy-start
  9.0 0.0 copy-done.1
  9.0 9.8 %ramp_fit.1.ramp_ref = bf16[64,64,96]{2,1,0:T(8,128)(2,1)S(1)} custom-call(bf16[64,64,512]{2,1,0:T(8,128)(2,1)S(1)} %bitcast.11, bf16[64,1,512]{2,1,0:T(2,128)(2,1)S(1)} %convert_element_type.46.weight_ref, bf16[512,64]{1,0:T(8,128)(2,1)S(1)} %copy.13.basis_ref, bf16[1024,1024]{1,0:T(8,128)(2,1)S(1)} %copy-done.1, f32[64,32]{1,0:T(8,128)S(1)} %fusion.17.row_ref), custom_call_target="tpu_custom_call" | custom-call | tf_op jit(solution)/shard_map/ramp_fit/pallas_call | solution.py:306
  18.7 0.0 copy-done
  18.8 124.8 %line_sums.1 = (f32[4,256,512]{2,1,0:T(8,128)}, bf16[64,64,512]{2,1,0:T(8,128)(2,1)}) custom-call(bf16[64,64,512]{2,1,0:T(8,128)(2,1)} %bitcast.12, bf16[64,64,96]{2,1,0:T(8,128)(2,1)S(1)} %ramp_fit.1.ramp_ref, bf16[96,512]{1,0:T(8,128)(2,1)S(1)} %maximum_bitcast_fusion.basis_ref, bf16[256,256]{1,0:T(8,128)(2,1)S(1)} %get-tuple-element.11.own_ref, ...), custom_call_target="tpu_custom_call" | custom-call | tf_op jit(solution)/shard_map/line_sums/pallas_call | solution.py:236
  143.6 0.0 copy-start.2
  143.6 4.4 %copy.14 = f32[256,4,512]{2,1,0:T(4,128)} copy(f32[256,4,512]{2,0,1:T(8,128)} %bitcast.14) | data formatting | bytes 4194304
  148.0 0.0 copy-done.2
  148.0 4.4 %copy.15 = bf16[64,64,512]{2,1,0:T(8,128)(2,1)} copy(bf16[64,64,512]{2,0,1:T(8,128)(2,1)S(1)} %bitcast.13) | data formatting | bytes 8388608
  (5 shorter events, 0.0 us)
Async XLA Ops:
  4.2 4.7 %copy-start.1 = (bf16[1024,1024]{1,0:T(8,128)(2,1)S(1)}, bf16[1024,1024]{1,0:T(8,128)(2,1)}, u32[]{:S(2)}) copy-start(bf16[1024,1024]{1,0:T(8,128)(2,1)} %inverse_ref.1) | copy-start | bytes 6291460
  8.9 9.8 %copy-start = (bf16[64,64,512]{2,0,1:T(8,128)(2,1)}, bf16[64,64,512]{2,0,1:T(8,128)(2,1)S(1)}, u32[]{:S(2)}) copy-start(bf16[64,64,512]{2,0,1:T(8,128)(2,1)S(1)} %copy.17) | copy-start | bytes 12582916
  143.6 4.4 %copy-start.2 = (bf16[64,64,512]{2,1,0:T(8,128)(2,1)S(1)}, bf16[64,64,512]{2,1,0:T(8,128)(2,1)}, u32[]{:S(2)}) copy-start(bf16[64,64,512]{2,1,0:T(8,128)(2,1)} %get-tuple-element.5) | copy-start | bytes 12582916

commit v4 on v3

--- a/solution.py
+++ b/solution.py
@@ -12,8 +12,9 @@
 PLANE = 4
 LINE = 4
 PARTS = 2
-LEAD = 4
-SKEW = 3
+LEAD = 3
+SKEW = 2
+TAIL = 6
 
 highest = lax.Precision.HIGHEST
 f32 = jnp.float32
@@ -99,7 +100,7 @@
 
     def raw_copy(k, p):
         return pltpu.make_async_remote_copy(
-            src_ref=corr.at[k, p - 1],
+            src_ref=corr.at[k, peer(p)],
             dst_ref=raw.at[k, pl.ds(pl.multiple_of(q * count, count), count), :],
             send_sem=raw_ss.at[k, p - 1], recv_sem=raw_rs.at[k, p - 1],
             device_id={"ifg": z * PLANE + peer(p)}, device_id_type=MESH)
@@ -133,16 +134,17 @@
         return jnp.dot(a, b, preferred_element_type=f32)
 
     def produce(k):
-        for p in range(1, PLANE + 1):
-            row, col = place(k, peer(p))
-            part = pl.ds(pl.multiple_of(col, width), width)
-            ramp = dot(ramp_ref[row], basis_ref[:, part])
-            corrected = (phase_ref[row, :, part].astype(f32) - ramp).astype(bf16)
-            if p == PLANE:
-                raw[k, pl.ds(pl.multiple_of(q * count, count), count), :] = corrected
-            else:
-                corr[k, p - 1] = corrected
-                raw_copy(k, p).start()
+        part = pl.ds(pl.multiple_of((k % PARTS) * width, width), width)
+        lines = ramp_ref[pl.ds((k // PARTS) * PLANE, PLANE)].reshape(PLANE * count, -1)
+        ramp = dot(lines, basis_ref[:, part])
+        for owner in range(PLANE):
+            row, _ = place(k, owner)
+            corr[k, owner] = (
+                phase_ref[row, :, part].astype(f32) - ramp[owner * count:(owner + 1) * count]
+            ).astype(bf16)
+        for p in range(1, PLANE):
+            raw_copy(k, p).start()
+        raw[k, pl.ds(pl.multiple_of(q * count, count), count), :] = corr[k, q]
 
     @pl.loop(0, LEAD)
     def _(k):
@@ -151,9 +153,10 @@
     def finish(k, total):
         row, col = place(k, q)
 
-        @pl.when((k // PARTS) // share == z)
-        def _():
-            disp[(k // PARTS) % share, :, pl.ds(pl.multiple_of(col, width), width)] = total
+        for j in range(share):
+            @pl.when(k // PARTS == z * share + j)
+            def _():
+                disp[:, j, pl.ds(pl.multiple_of(col, width), width)] = total
 
         high = total.astype(bf16)
         low = (total - high.astype(f32)).astype(bf16)
@@ -164,7 +167,7 @@
         resid[row, :, pl.ds(pl.multiple_of(col, width), width)] = res_send[
             k, pl.ds(pl.multiple_of(q * count, count), count), :]
 
-    @pl.loop(0, chunks + 2 * SKEW)
+    @pl.loop(0, chunks + TAIL)
     def _(t):
         @pl.when(t + LEAD < chunks)
         def _():
@@ -201,9 +204,9 @@
             line_copy(back_send, far, far_ss.at[1], far_rs, k, beside).start()
             finish(k, rest + out_part[slot])
 
-        @pl.when((is_inner == 0) & (t >= 2 * SKEW))
-        def _():
-            k = t - 2 * SKEW
+        @pl.when((is_inner == 0) & (t >= TAIL))
+        def _():
+            k = t - TAIL
             line_copy(back_send, far, far_ss.at[1], far_rs, k, beside).wait_recv()
             finish(k, far[k].astype(f32) + dot(own_ref[...], raw[k]))
 
@@ -236,12 +239,12 @@
     return pl.pallas_call(
         line_kernel,
         out_shape=(
-            jax.ShapeDtypeStruct((share, dates, cols), f32),
+            jax.ShapeDtypeStruct((dates, share, cols), f32),
             jax.ShapeDtypeStruct((rows, count, cols), bf16),
         ),
         in_specs=[vmem] * 6,
         out_specs=(vmem, vmem),
-        scratch_shapes=[pltpu.VMEM((chunks, PLANE - 1, count, width), bf16)] + [pltpu.VMEM((SKEW + 1, dates, width), f32)] * 2 + [slots] * 6 + [
+        scratch_shapes=[pltpu.VMEM((chunks, PLANE, count, width), bf16)] + [pltpu.VMEM((SKEW + 1, dates, width), f32)] * 2 + [slots] * 6 + [
             sems((chunks, PLANE - 1)), sems((chunks, PLANE - 1)),
             sems((chunks,)), sems((chunks,)),
             sems((2, chunks)), sems((chunks,)),
@@ -297,7 +300,9 @@
                 line += row_ref[r, base + d] * coef[base + d]
             top = line.astype(bf16)
             rest = (line - top.astype(f32)).astype(bf16)
-            rows_out[r] = jnp.concatenate([top, top, rest], 1)
+            share = rows // (PLANE * LINE)
+            turn = r // (share * PLANE) * share + r % share
+            rows_out[turn * PLANE + r // share % PLANE] = jnp.concatenate([top, top, rest], 1)
 
 
 def ramp_call(by_row, weight, basis, ramp_inverse, row_basis):
@@ -344,7 +349,7 @@
         by_row, ramp_rows,
         jnp.concatenate([high, low, high], 1).T,
         own, outer, pair)
-    return displacement.transpose(1, 0, 2), residual.transpose(1, 0, 2)
+    return displacement, residual.transpose(1, 0, 2)
 
 
 def solution(mesh):

time: 153 us -> 150 us (0.980)
  Pallas kernels: 135 us -> 132 us
    pallas_call x1, Pallas kernels: 125 us -> 122 us  [line_call(): pl.pallas_call(line_kernel, out_shape=(jax.ShapeDtypeStruct((dates, share...]
where the time goes in v4:
time: 150 us; the launch traced here: 149 us
  Pallas kernels  132 us (88%)
  local copies, waits for them, and re-layouts  15.1 us (10%)
    pallas_call x1, Pallas kernels, line_call(): pl.pallas_call(line_kernel, out_shape=(jax.ShapeDtypeStruct((dates, share...  122 us
    unnamed x9, local copies, waits for them, and re-layouts  12.7 us
    pallas_call x1, Pallas kernels, ramp_call(): pl.pallas_call(ramp_kernel, out_shape=jax.ShapeDtypeStruct((rows, count,...  9.99 us

profile of v4, /device:TPU:1, one launch (start us, length us, event | category | flops | bytes accessed | tf_op | source)
XLA Modules:
  0.0 149.2 jit_solution(18418783642362679220)
XLA Ops:
  0.7 0.7 convert_convert_fusion
  1.4 0.8 fusion.21
  2.2 0.1 fusion.17.row_ref
  2.3 0.1 reduce-precision_convert_fusion
  2.5 0.1 copy.12.basis_ref
  2.6 0.1 subtract_convert_fusion.pair_ref
  2.7 1.0 constant_dynamic-slice_fusion.1
  3.8 0.1 broadcast_in_dim.10
  3.9 0.3 convert_element_type.46.weight_ref
  4.2 0.0 copy-start.1
  4.3 4.7 %copy.15 = bf16[64,64,512]{2,0,1:T(8,128)(2,1)S(1)} copy(bf16[64,64,512]{2,1,0:T(8,128)(2,1)} %param.5) | data formatting | bytes 8388608 | tf_op args[0]
  8.9 0.0 copy-start
  9.0 0.0 copy-done.1
  9.0 10.0 %ramp_fit.1.ramp_ref = bf16[64,64,96]{2,1,0:T(8,128)(2,1)S(1)} custom-call(bf16[64,64,512]{2,1,0:T(8,128)(2,1)S(1)} %bitcast.10, bf16[64,1,512]{2,1,0:T(2,128)(2,1)S(1)} %convert_element_type.46.weight_ref, bf16[512,64]{1,0:T(8,128)(2,1)S(1)} %copy.12.basis_ref, bf16[1024,1024]{1,0:T(8,128)(2,1)S(1)} %copy-done.1, f32[64,32]{1,0:T(8,128)S(1)} %fusion.17.row_ref), custom_call_target="tpu_custom_call" | custom-call | tf_op jit(solution)/shard_map/ramp_fit/pallas_call | solution.py:311
  19.0 0.0 copy-done
  19.0 122.2 %line_sums.1 = (f32[256,4,512]{2,1,0:T(4,128)}, bf16[64,64,512]{2,1,0:T(8,128)(2,1)}) custom-call(bf16[64,64,512]{2,1,0:T(8,128)(2,1)} %bitcast.11, bf16[64,64,96]{2,1,0:T(8,128)(2,1)S(1)} %ramp_fit.1.ramp_ref, bf16[96,512]{1,0:T(8,128)(2,1)S(1)} %maximum_bitcast_fusion.basis_ref, bf16[256,256]{1,0:T(8,128)(2,1)S(1)} %get-tuple-element.11.own_ref, ...), custom_call_target="tpu_custom_call" | custom-call | tf_op jit(solution)/shard_map/line_sums/pallas_call | solution.py:239
  141.2 0.0 copy-start.2
  141.2 6.7 %copy.13 = bf16[64,64,512]{2,1,0:T(8,128)(2,1)} copy(bf16[64,64,512]{2,0,1:T(8,128)(2,1)} %bitcast.12) | data formatting | bytes 8388608
  147.9 0.0 copy-done.2
  147.9 1.3 copy.17
  (5 shorter events, 0.0 us)
Async XLA Ops:
  4.2 4.7 %copy-start.1 = (bf16[1024,1024]{1,0:T(8,128)(2,1)S(1)}, bf16[1024,1024]{1,0:T(8,128)(2,1)}, u32[]{:S(2)}) copy-start(bf16[1024,1024]{1,0:T(8,128)(2,1)} %inverse_ref.1) | copy-start | bytes 6291460
  8.9 10.0 %copy-start = (bf16[64,64,512]{2,0,1:T(8,128)(2,1)}, bf16[64,64,512]{2,0,1:T(8,128)(2,1)S(1)}, u32[]{:S(2)}) copy-start(bf16[64,64,512]{2,0,1:T(8,128)(2,1)S(1)} %copy.15) | copy-start | bytes 12582916
  141.2 6.7 %copy-start.2 = (f32[256,4,512]{2,1,0:T(4,128)S(1)}, f32[256,4,512]{2,1,0:T(4,128)}, u32[]{:S(2)}) copy-start(f32[256,4,512]{2,1,0:T(4,128)} %get-tuple-element.18) | copy-start | bytes 6291460

commit v5 on v4

--- a/solution.py
+++ b/solution.py
@@ -12,9 +12,9 @@
 PLANE = 4
 LINE = 4
 PARTS = 2
-LEAD = 3
+LEAD = 2
 SKEW = 2
-TAIL = 6
+TAIL = 5
 
 highest = lax.Precision.HIGHEST
 f32 = jnp.float32

time: 150 us -> 150 us (level)
  no operation moved by 1% of the time
where the time goes in v5:
time: 150 us; the launch traced here: 149 us
  Pallas kernels  132 us (88%)
  local copies, waits for them, and re-layouts  15.1 us (10%)
    pallas_call x1, Pallas kernels, line_call(): pl.pallas_call(line_kernel, out_shape=(jax.ShapeDtypeStruct((dates, share...  122 us
    unnamed x9, local copies, waits for them, and re-layouts  12.7 us
    pallas_call x1, Pallas kernels, ramp_call(): pl.pallas_call(ramp_kernel, out_shape=jax.ShapeDtypeStruct((rows, count,...  9.99 us

profile of v5, /device:TPU:1, one launch (start us, length us, event | category | flops | bytes accessed | tf_op | source)
XLA Modules:
  0.0 149.2 jit_solution(12323625395864364320)
XLA Ops:
  0.7 0.7 convert_convert_fusion
  1.4 0.8 fusion.21
  2.2 0.1 fusion.17.row_ref
  2.3 0.1 reduce-precision_convert_fusion
  2.5 0.1 copy.12.basis_ref
  2.6 0.1 subtract_convert_fusion.pair_ref
  2.7 1.0 constant_dynamic-slice_fusion.1
  3.8 0.1 broadcast_in_dim.10
  3.9 0.3 convert_element_type.46.weight_ref
  4.2 0.0 copy-start.1
  4.3 4.7 %copy.15 = bf16[64,64,512]{2,0,1:T(8,128)(2,1)S(1)} copy(bf16[64,64,512]{2,1,0:T(8,128)(2,1)} %param.5) | data formatting | bytes 8388608 | tf_op args[0]
  8.9 0.0 copy-start
  9.0 0.0 copy-done.1
  9.0 10.0 %ramp_fit.1.ramp_ref = bf16[64,64,96]{2,1,0:T(8,128)(2,1)S(1)} custom-call(bf16[64,64,512]{2,1,0:T(8,128)(2,1)S(1)} %bitcast.10, bf16[64,1,512]{2,1,0:T(2,128)(2,1)S(1)} %convert_element_type.46.weight_ref, bf16[512,64]{1,0:T(8,128)(2,1)S(1)} %copy.12.basis_ref, bf16[1024,1024]{1,0:T(8,128)(2,1)S(1)} %copy-done.1, f32[64,32]{1,0:T(8,128)S(1)} %fusion.17.row_ref), custom_call_target="tpu_custom_call" | custom-call | tf_op jit(solution)/shard_map/ramp_fit/pallas_call | solution.py:311
  19.0 0.0 copy-done
  19.0 122.2 %line_sums.1 = (f32[256,4,512]{2,1,0:T(4,128)}, bf16[64,64,512]{2,1,0:T(8,128)(2,1)}) custom-call(bf16[64,64,512]{2,1,0:T(8,128)(2,1)} %bitcast.11, bf16[64,64,96]{2,1,0:T(8,128)(2,1)S(1)} %ramp_fit.1.ramp_ref, bf16[96,512]{1,0:T(8,128)(2,1)S(1)} %maximum_bitcast_fusion.basis_ref, bf16[256,256]{1,0:T(8,128)(2,1)S(1)} %get-tuple-element.11.own_ref, ...), custom_call_target="tpu_custom_call" | custom-call | tf_op jit(solution)/shard_map/line_sums/pallas_call | solution.py:239
  141.2 0.0 copy-start.2
  141.2 6.7 %copy.13 = bf16[64,64,512]{2,1,0:T(8,128)(2,1)} copy(bf16[64,64,512]{2,0,1:T(8,128)(2,1)} %bitcast.12) | data formatting | bytes 8388608
  147.9 0.0 copy-done.2
  147.9 1.3 copy.17
  (5 shorter events, 0.0 us)
Async XLA Ops:
  4.2 4.7 %copy-start.1 = (bf16[1024,1024]{1,0:T(8,128)(2,1)S(1)}, bf16[1024,1024]{1,0:T(8,128)(2,1)}, u32[]{:S(2)}) copy-start(bf16[1024,1024]{1,0:T(8,128)(2,1)} %inverse_ref.1) | copy-start | bytes 6291460
  8.9 10.0 %copy-start = (bf16[64,64,512]{2,0,1:T(8,128)(2,1)}, bf16[64,64,512]{2,0,1:T(8,128)(2,1)S(1)}, u32[]{:S(2)}) copy-start(bf16[64,64,512]{2,0,1:T(8,128)(2,1)S(1)} %copy.15) | copy-start | bytes 12582916
  141.2 6.7 %copy-start.2 = (f32[256,4,512]{2,1,0:T(4,128)S(1)}, f32[256,4,512]{2,1,0:T(4,128)}, u32[]{:S(2)}) copy-start(f32[256,4,512]{2,1,0:T(4,128)} %get-tuple-element.18) | copy-start | bytes 6291460
